TPU v7x, 32 devices: a whole 2x2x4 slice. The times are simulated.
32 devices in a mesh: groups: 2 (over y), context: 2 (over x), expert: 4 (over z), tensor: 2 (over core).
Axes of the slice: x: 2, y: 2, z: 4, core: 2. Of those that a mesh axis runs over, the one named last changes fastest.
Arguments:
- queries: bfloat16 [2048, 2048], P(('groups', 'context', 'expert'), 'tensor'), parts along dimension 0, may hold values from -60 to 60
- keys: bfloat16 [2048, 512], P(('groups', 'context', 'expert'), 'tensor'), parts along dimension 0, may hold values from -5 to 5
- values: bfloat16 [2048, 512], P(('groups', 'context', 'expert'), 'tensor'), parts along dimension 0, may hold values from -6 to 6
- resid: bfloat16 [2048, 2048], P(('groups', 'context', 'expert'), 'tensor'), parts along dimension 0, may hold values from -200 to 200
- expert_out: bfloat16 [4, 4, 4, 80, 2048], P(('groups', 'context'), 'expert', None, None, 'tensor'), parts along dimension 0, may hold values from -6 to 6
- routes: int32 [2048, 2], P(('groups', 'context', 'expert')), parts along dimension 0, may hold values from 0 to 3, all different within a row; in each aligned block of 128 rows (0 to 127, 128 to 255, ...) at most 80 rows name the same one
- route_weights: float32 [2048, 2], P(('groups', 'context', 'expert')), parts along dimension 0, may hold values from 0.1 to 1
- pattern: int32 [8, 8], P(('context', 'expert')), may hold values from 0 to 1, as said below
- lengths: int32 [128], P('groups'), parts along dimension 0, may hold values from 1 to 256, 1024 in all
- teacher: float32 [128, 64], P('groups'), parts along dimension 0, may hold values from 0 to 1
- gain: float32 [2048], P('tensor'), may hold values from 0.5 to 1.5
- head_weight: float32 [2048, 64], P('tensor'), may hold values from -0.125 to 0.125
Outputs:
- grad_query: bfloat16 [2048, 2048], P(('groups', 'context', 'expert'), 'tensor'), parts along dimension 0
- grad_key: float32 [2048, 512], P(('groups', 'context', 'expert'), 'tensor'), parts along dimension 0
- value_gradient: float32 [2048, 512], P(('groups', 'context', 'expert'), 'tensor'), parts along dimension 0
- grad_expert: bfloat16 [4, 4, 4, 80, 2048], P(('groups', 'context'), 'expert', None, None, 'tensor'), parts along dimension 0
There are 2 independent parts, one for each index of `groups`. A program takes and returns all parts, laid end to end along the dimension named above; an argument that names none is the same for every part. Nothing has to cross between parts.
Inputs may be any that keep to these rules, and one draw needn't show every extreme that they name: `pattern`: entry (i, i) is 1; entry (i, j) for i != j is 0 unless i XOR j is a power of two. `routes`: each row names 2 different experts; at most 80 of the pairs of the rows of one device name one expert.
All inputs are finite; a program needn't handle non-finite values.
Results may differ from a plain program's by a relative error of at most 0.0058.
Values may be sent and summed in bfloat16 or wider, within the bound.
A program may use at most 64 MiB of HBM per device.

v0:
```python
import jax
import jax.numpy as jnp
from jax import lax
from jax.sharding import PartitionSpec as P

BLOCK_POSITIONS = 128
HEAD_FEATURES = 128
LOSS_SCALE = 256
D = 2048


EPSILON = 1e-05
NEGATIVE = -1e30
HIGHEST_PRECISION = lax.Precision.HIGHEST


def swapped(array, axis, distance):
    return lax.ppermute(array, axis, [(i, i ^ 1 << distance) for i in range(lax.axis_size(axis))])


def block_probs(query_block, key_set, key_keep, score_scale):
    scores = (
        jnp.einsum("qkgd,skd->kgqs", query_block, key_set, preferred_element_type=jnp.float32)
        * score_scale
    )
    scores = jnp.where(key_keep[None, None, None, :], scores, NEGATIVE)
    row_max = jnp.max(scores, axis=-1, keepdims=True)
    raised = jnp.exp(scores - row_max)
    return raised / jnp.sum(raised, axis=-1, keepdims=True)


def local(
    queries,
    keys,
    values,
    resid,
    expert_out,
    routes,
    route_weights,
    pattern,
    lengths,
    teacher,
    gain,
    head_weight,
):
    shard_bits = lax.axis_size(("context", "expert")).bit_length() - 1
    shard_id = lax.axis_index(("context", "expert"))
    tok_dev = queries.shape[0]
    blocks = tok_dev // BLOCK_POSITIONS
    device_levels = blocks.bit_length() - 1
    kv_dev = keys.shape[1] // HEAD_FEATURES
    heads_dev = queries.shape[1] // HEAD_FEATURES
    group_size = heads_dev // kv_dev
    row_width = queries.shape[1]
    kv_width = keys.shape[1]
    score_scale = HEAD_FEATURES ** (-0.5)
    q_blocks = queries.reshape(blocks, BLOCK_POSITIONS, kv_dev, group_size, HEAD_FEATURES)
    key_rows = keys.reshape(blocks, BLOCK_POSITIONS, kv_width)
    value_rows = values.reshape(blocks, BLOCK_POSITIONS, kv_width)
    received = [
        swapped((keys, values), ("context", "expert"), level_bit) for level_bit in range(shard_bits)
    ]

    def key_value_sets(partner_pairs, block_position):
        key_list = [key_rows[block_position]] + [
            key_rows[block_position ^ 1 << level] for level in range(device_levels)
        ]
        value_list = [value_rows[block_position]] + [
            value_rows[block_position ^ 1 << level] for level in range(device_levels)
        ]
        key_list = key_list + [
            pair[0].reshape(blocks, BLOCK_POSITIONS, kv_width)[block_position]
            for pair in partner_pairs
        ]
        value_list = value_list + [
            pair[1].reshape(blocks, BLOCK_POSITIONS, kv_width)[block_position]
            for pair in partner_pairs
        ]
        key_set = jnp.concatenate(key_list, axis=0).reshape(-1, kv_dev, HEAD_FEATURES)
        value_set = jnp.concatenate(value_list, axis=0).reshape(-1, kv_dev, HEAD_FEATURES)
        return (key_set, value_set)

    def block_flags(block_position):
        partners = [
            shard_id * blocks + (block_position ^ 1 << level) for level in range(device_levels)
        ]
        partners = partners + [
            jnp.bitwise_xor(shard_id, 1 << level_bit) * blocks + block_position
            for level_bit in range(shard_bits)
        ]
        flag_bits = jnp.stack(
            [jnp.int32(1)] + [pattern[block_position, partner] for partner in partners]
        )
        return jnp.repeat(flag_bits, BLOCK_POSITIONS) > 0

    block_position = 0
    key_set, value_set = key_value_sets(received, block_position)
    attn_prob = block_probs(
        q_blocks[block_position], key_set, block_flags(block_position), score_scale
    )
    prob_list = [attn_prob]
    block_out = jnp.einsum(
        "kgqs,skd->qkgd",
        attn_prob.astype(jnp.bfloat16),
        value_set,
        preferred_element_type=jnp.float32,
    )
    attn_list = block_out.reshape(BLOCK_POSITIONS, row_width)
    experts = expert_out.shape[2]
    capacity = expert_out.shape[3]
    arrived = lax.all_to_all(expert_out, "expert", split_axis=2, concat_axis=1, tiled=True)
    flat_rows = arrived.reshape(experts * capacity, -1)
    pair_routes = routes.reshape(-1)
    onehot = (pair_routes[:, None] == jnp.arange(experts, dtype=jnp.int32)[None, :]).astype(
        jnp.int32
    )
    slot_rank = jnp.sum((jnp.cumsum(onehot, axis=0) - onehot) * onehot, axis=1)
    flat_index = pair_routes * capacity + slot_rank
    picked = (
        jnp.take(flat_rows, flat_index, axis=0)
        .astype(jnp.float32)
        .reshape(tok_dev, routes.shape[1], -1)
    )
    mixture = jnp.sum(route_weights[:, :, None] * picked, axis=1)
    hidden = resid.astype(jnp.float32) + attn_list + mixture
    square_sum = lax.psum(jnp.sum(hidden * hidden, axis=1), "tensor")
    row_rms = jnp.sqrt(square_sum / D + EPSILON)
    normed = hidden / row_rms[:, None] * gain
    logits = lax.psum(jnp.dot(normed, head_weight, precision=HIGHEST_PRECISION), "tensor")
    turn_ends = jnp.cumsum(lengths)
    position = shard_id * tok_dev + jnp.arange(tok_dev, dtype=jnp.int32)
    turn_id = jnp.sum((turn_ends[None, :] <= position[:, None]).astype(jnp.int32), axis=1)
    turn_pick = (turn_id[:, None] == jnp.arange(lengths.shape[0], dtype=jnp.int32)[None, :]).astype(
        jnp.float32
    )
    target = jnp.dot(turn_pick, teacher, precision=HIGHEST_PRECISION)
    grad_logit = (jax.nn.sigmoid(logits) - target) * LOSS_SCALE
    grad_normed = jnp.dot(grad_logit, head_weight.T, precision=HIGHEST_PRECISION)
    inner_sum = lax.psum(jnp.sum(grad_normed * gain * hidden, axis=1), "tensor")
    grad_hidden = (
        gain * grad_normed / row_rms[:, None] - hidden * (inner_sum / (D * row_rms**3))[:, None]
    )
    grad_out = grad_hidden.astype(jnp.bfloat16).reshape(
        blocks, BLOCK_POSITIONS, kv_dev, group_size, HEAD_FEATURES
    )
    own_key = jnp.zeros((blocks, BLOCK_POSITIONS, kv_width), jnp.float32)
    local_value = jnp.zeros((blocks, BLOCK_POSITIONS, kv_width), jnp.float32)
    send_key = [[] for level_bit in range(shard_bits)]
    outgoing_value = [[] for level_bit in range(shard_bits)]
    block_position = 0
    key_set, value_set = key_value_sets(received, block_position)
    attn_prob = prob_list[block_position]
    weight_rows = attn_prob.astype(jnp.bfloat16)
    grad_prob = jnp.einsum(
        "qkgd,skd->kgqs", grad_out[block_position], value_set, preferred_element_type=jnp.float32
    )
    value_set_gradient = jnp.einsum(
        "rcnw,nrco->wro", weight_rows, grad_out[block_position], preferred_element_type=jnp.float32
    ).reshape(-1, BLOCK_POSITIONS, kv_width)
    row_delta = jnp.sum(attn_prob * grad_prob, axis=-1, keepdims=True)
    grad_score = (attn_prob * (grad_prob - row_delta) * score_scale).astype(jnp.bfloat16)
    grad_query = jnp.einsum(
        "kgqs,skd->qkgd", grad_score, key_set, preferred_element_type=jnp.float32
    )
    grad_rows = grad_query.reshape(BLOCK_POSITIONS, row_width).astype(jnp.bfloat16)
    grad_kset = jnp.einsum(
        "rcnw,nrco->wro", grad_score, q_blocks[block_position], preferred_element_type=jnp.float32
    ).reshape(-1, BLOCK_POSITIONS, kv_width)
    own_key = own_key.at[block_position].add(grad_kset[0])
    local_value = local_value.at[block_position].add(value_set_gradient[0])
    for level_bit in range(shard_bits):
        send_key[level_bit].append(grad_kset[1 + device_levels + level_bit])
        outgoing_value[level_bit].append(value_set_gradient[1 + device_levels + level_bit])
    for level_bit in range(shard_bits):
        back_key, back_value = (
            swapped(
                jnp.stack(send_key[level_bit]).astype(jnp.bfloat16),
                ("context", "expert"),
                level_bit,
            ).astype(jnp.float32),
            swapped(
                jnp.stack(outgoing_value[level_bit]).astype(jnp.bfloat16),
                ("context", "expert"),
                level_bit,
            ).astype(jnp.float32),
        )
        own_key = own_key + back_key
        local_value = local_value + back_value
    contrib = (
        (route_weights[:, :, None] * grad_hidden[:, None, :])
        .astype(jnp.bfloat16)
        .reshape(-1, grad_hidden.shape[1])
    )
    buffer = (
        jnp.zeros((experts * capacity, grad_hidden.shape[1]), jnp.bfloat16)
        .at[flat_index]
        .set(contrib)
    )
    grad_expert = lax.all_to_all(
        buffer.reshape(1, experts, 1, capacity, -1),
        "expert",
        split_axis=1,
        concat_axis=2,
        tiled=True,
    )
    return (
        grad_rows,
        own_key.reshape(tok_dev, kv_width),
        local_value.reshape(tok_dev, kv_width),
        grad_expert,
    )


def solution(mesh):
    placed = (
        P(("groups", "context", "expert"), "tensor"),
        P(("groups", "context", "expert"), "tensor"),
        P(("groups", "context", "expert"), "tensor"),
        P(("groups", "context", "expert"), "tensor"),
        P(("groups", "context"), "expert", None, None, "tensor"),
        P(("groups", "context", "expert"), None),
        P(("groups", "context", "expert"), None),
        P(("context", "expert"), None),
        P("groups"),
        P("groups", None),
        P("tensor"),
        P("tensor", None),
    )
    return jax.shard_map(
        local,
        mesh=mesh,
        in_specs=placed,
        out_specs=(
            P(("groups", "context", "expert"), "tensor"),
            P(("groups", "context", "expert"), "tensor"),
            P(("groups", "context", "expert"), "tensor"),
            P(("groups", "context"), "expert", None, None, "tensor"),
        ),
        check_vma=False,
    )
```

profile of v0, /device:TPU:0, one launch (start us, length us, event | category | flops | bytes accessed | tf_op | source)
XLA Modules:
  0.0 86.3 jit_solution(17052111443029709541)
XLA Ops:
  0.7 1.0 %copy.146 = bf16[128,256]{0,1:T(8,128)(2,1)S(1)} copy(bf16[128,256]{1,0:T(8,128)(2,1)} %param.17) | data formatting | bytes 131072 | tf_op args[1]
  1.7 3.0 %collective-permute-start.2 = (bf16[128,256]{0,1:T(8,128)(2,1)S(1)}, bf16[128,256]{0,1:T(8,128)(2,1)S(1)}, u32[]{:S(2)}, u32[]{:S(2)}) collective-permute-start(bf16[128,256]{0,1:T(8,128)(2,1)S(1)} %copy.146), channel_id=1, source_target_pairs={{0,8},{2,10},{4,12},{6,14},{8,0},{10,2},{12,4},{14,6},{1,9},{3,11}... | collective-permute-start | bytes 196616 | tf_op jit(solution)/shard_map/ppermute | solution.py:18
  4.7 2.6 %collective-permute-start.1 = (bf16[128,256]{0,1:T(8,128)(2,1)S(1)}, bf16[128,256]{0,1:T(8,128)(2,1)S(1)}, u32[]{:S(2)}, u32[]{:S(2)}) collective-permute-start(bf16[128,256]{0,1:T(8,128)(2,1)S(1)} %copy.146), channel_id=1, source_target_pairs={{0,4},{2,6},{4,0},{6,2},{8,12},{10,14},{12,8},{14,10},{1,5},{3,7},... | collective-permute-start | bytes 196616 | tf_op jit(solution)/shard_map/ppermute | solution.py:18
  7.3 0.3 collective-permute-start.4
  7.6 1.6 %collective-permute-start.3 = (bf16[128,256]{1,0:T(8,128)(2,1)}, bf16[128,256]{1,0:T(8,128)(2,1)S(1)}, u32[]{:S(2)}, u32[]{:S(2)}) collective-permute-start(bf16[128,256]{1,0:T(8,128)(2,1)} %param.18), channel_id=1, source_target_pairs={{0,2},{2,0},{4,6},{6,4},{8,10},{10,8},{12,14},{14,12},{1,3},{3,1},... | collective-permute-start | bytes 196616 | tf_op jit(solution)/shard_map/ppermute | solution.py:18
  9.2 0.5 collective-permute-start.5
  9.7 3.9 %all-to-all-start = ((bf16[1,1,4,80,1024]{4,3,1,0,2:T(8,128)(2,1)}), bf16[1,1,4,80,1024]{4,3,1,0,2:T(8,128)(2,1)S(1)}, u32[]{:S(2)}, u32[]{:S(2)}) async-start(bf16[1,1,4,80,1024]{4,3,1,0,2:T(8,128)(2,1)} %bitcast.132), calls=%async_computation | async-start | bytes 1310720 | tf_op jit(solution)/shard_map/all_to_all | solution.py:111
  13.6 0.7 broadcast_multiply_fusion
  14.3 0.8 copy.153
  15.4 1.4 %constant_dynamic-slice_fusion.2 = (s32[1,1]{1,0:T(1,128)}, s32[1,1]{1,0:T(1,128)}, s32[1,1]{1,0:T(1,128)}) fusion(s32[1,8]{1,0:T(1,128)} %param.23, s32[]{:T(128)S(6)} %select_n.39, s32[]{:T(128)S(6)} %select_n.41, s32[]{:T(128)S(6)} %select_n.40), kind=kLoop, calls=%fused_computation.66 | loop fusion | bytes 36 | tf_op jit(solution)/shard_map/dynamic_slice | solution.py:92
  16.7 2.0 %add_compare_fusion = pred[4]{0:T(512)(128)(4,1)S(1)} fusion(s32[1]{0:T(128)} %bitcast.5, s32[1]{0:T(128)} %bitcast.4, s32[1]{0:T(128)} %bitcast.3, s32[1]{0:T(128)} %constant.90.clone.1), kind=kLoop, calls=%fused_computation.69 | loop fusion | flops 16 | bytes 20 | tf_op jit(solution)/shard_map/gt | solution.py:94
  18.8 0.7 copy.161
  20.0 0.8 copy.152
  21.0 1.2 %reduce-window.18 = s32[4,2,128]{2,1,0:T(2,128)S(1)} reduce-window(s32[4,2,128]{2,1,0:T(2,128)S(1)} %compare_convert_fusion, s32[]{:T(128)} %constant.91.clone.1), window={size=1x1x128 pad=0_0x0_0x127_0}, to_apply=%region_2.3 | reduce-window | flops 130048 | bytes 8196 | tf_op jit(solution)/shard_map/reduce-window
  23.3 2.1 %collective-permute-start = (bf16[128,256]{0,1:T(8,128)(2,1)S(1)}, bf16[128,256]{0,1:T(8,128)(2,1)S(1)}, u32[]{:S(2)}, u32[]{:S(2)}) collective-permute-start(bf16[128,256]{0,1:T(8,128)(2,1)S(1)} %copy.146), channel_id=1, source_target_pairs={{0,2},{2,0},{4,6},{6,4},{8,10},{10,8},{12,14},{14,12},{1,3},{3,1},... | collective-permute-start | bytes 196616 | tf_op jit(solution)/shard_map/ppermute | solution.py:18
  25.6 4.2 %collective-permute-done = bf16[128,256]{0,1:T(8,128)(2,1)S(1)} collective-permute-done((bf16[128,256]{0,1:T(8,128)(2,1)S(1)}, bf16[128,256]{0,1:T(8,128)(2,1)S(1)}, u32[]{:S(2)}, u32[]{:S(2)}) %collective-permute-start) | collective-permute-done | bytes 65568 | tf_op jit(solution)/shard_map/ppermute | solution.py:18
  29.8 2.2 %fusion.42 = (f32[2,4,128]{2,1,0:T(4,128)S(1)}, f32[2,4,128,512]{2,3,1,0:T(8,128)}) fusion(pred[512]{0:T(512)(128)(4,1)S(1)} %broadcast_bitcast_fusion, bf16[512,2,128,1]{0,2,3,1:T(8,128)(2,1)S(1)} %bitcast.138, bf16[128,2,4,128]{0,3,2,1:T(8,128)(2,1)S(1)} %bitcast.136), kind=kOutput, calls=%fused_computation.82 | convolution fusion | flops 136315392 | bytes 2626048 | tf_op jit(solution)/shard_map/sub | solution.py:28
  32.0 1.9 %fusion.20 = f32[2,128,4,128]{3,1,2,0:T(8,128)S(1)} fusion(bf16[512,2,128,1]{0,2,3,1:T(8,128)(2,1)S(1)} %bitcast.128, f32[2,4,128,512]{2,3,1,0:T(8,128)} %get-tuple-element.62, f32[2,4,128]{2,1,0:T(4,128)S(1)} %get-tuple-element.61), kind=kOutput, calls=%fused_computation.38 | convolution fusion | flops 135266304 | bytes 2887680 | tf_op jit(solution)/shard_map/kgqs,skd->qkgd/dot_general | solution.py:102
  34.2 1.2 %gather_fusion = bf16[256,1024]{1,0:T(8,128)(2,1)S(1)} fusion(bf16[320,1024]{1,0:T(8,128)(2,1)S(1)} %bitcast.126, s32[1024]{0:T(1024)S(1)} %pad_clamp_fusion), kind=kCustom, calls=%fused_computation | custom fusion | bytes 1049600 | tf_op jit(solution)/shard_map/jit(_take)/gather | solution.py:120
  35.3 0.2 gather.7
  35.6 1.7 %multiply_reduce_fusion = f32[128,1024]{1,0:T(8,128)S(1)} fusion(bf16[128,2,1024]{2,1,0:T(2,128)(2,1)S(1)} %gather.7, pred[128,2]{1,0:T(8,128)(4,1)S(1)} %copy.158, f32[128,2]{1,0:T(8,128)S(1)} %copy.152), kind=kLoop, calls=%fused_computation.21 | loop fusion | flops 917504 | bytes 1049856 | tf_op jit(solution)/shard_map/reduce_sum | solution.py:124
  37.4 2.5 %psum.21 = f32[128]{0:T(128)S(1)} all-reduce(f32[128]{0:T(128)S(1)} %get-tuple-element.50), channel_id=1, replica_groups=mesh['groups'=2,'context'=2,'expert'=4,'tensor'=2] {'tensor'}, use_global_device_ids=true, to_apply=%region_7.8 | all-reduce | flops 128 | bytes 1024 | tf_op jit(solution)/shard_map/psum | solution.py:126
  39.9 0.7 fusion.16
  40.7 3.4 %psum.22 = f32[128,64]{0,1:T(8,128)S(1)} all-reduce(f32[128,64]{0,1:T(8,128)S(1)} %fusion.16), channel_id=1, replica_groups=mesh['groups'=2,'context'=2,'expert'=4,'tensor'=2] {'tensor'}, use_global_device_ids=true, to_apply=%region_8.9 | all-reduce | flops 8192 | bytes 65536 | tf_op jit(solution)/shard_map/psum | solution.py:129
  44.1 0.3 fusion.9
  44.4 0.7 multiply_reduce_fusion.1
  45.1 2.5 %psum.23 = f32[128]{0:T(128)S(1)} all-reduce(f32[128]{0:T(128)S(1)} %get-tuple-element.63), channel_id=1, replica_groups=mesh['groups'=2,'context'=2,'expert'=4,'tensor'=2] {'tensor'}, use_global_device_ids=true, to_apply=%region_12.13 | all-reduce | flops 128 | bytes 1024 | tf_op jit(solution)/shard_map/psum | solution.py:139
  47.9 2.9 %fusion.44 = (bf16[512,2,128]{0,2,1:T(8,128)(2,1)S(1)}, f32[512,2,128]{0,2,1:T(8,128)}) fusion(bf16[128,2,4,128]{0,3,2,1:T(8,128)(2,1)S(1)} %bitcast.130, f32[2,4,128,512]{2,3,1,0:T(8,128)} %get-tuple-element.62, f32[2,4,128]{2,1,0:T(4,128)S(1)} %get-tuple-element.61), kind=kOutput, calls=%fused_computation.84 | convolution fusion | flops 135397376 | bytes 3149824 | tf_op jit(solution)/shard_map/rcnw,nrco->wro/dot_general | solution.py:157
  50.8 1.8 %fusion.45 = f32[2,512,128,4]{2,1,3,0:T(8,128)} fusion(bf16[512,2,128,1]{0,2,3,1:T(8,128)(2,1)S(1)} %bitcast.129, bf16[128,2,4,128]{0,3,2,1:T(8,128)(2,1)S(1)} %bitcast.131), kind=kOutput, calls=%fused_computation.85 | convolution fusion | flops 134217728 | bytes 2621440 | tf_op jit(solution)/shard_map/qkgd,skd->kgqs/dot_general | solution.py:154
  52.9 0.8 collective-permute-start.10
  53.8 1.5 %collective-permute-start.11 = (bf16[1,128,256]{2,1,0:T(8,128)(2,1)S(1)}, bf16[1,128,256]{2,1,0:T(8,128)(2,1)S(1)}, u32[]{:S(2)}, u32[]{:S(2)}) collective-permute-start(bf16[1,128,256]{2,1,0:T(8,128)(2,1)S(1)} %copy.176), channel_id=1, source_target_pairs={{0,8},{2,10},{4,12},{6,14},{8,0},{10,2},{12,4},{14,6},{1,9},{3,11}... | collective-permute-start | bytes 196616 | tf_op jit(solution)/shard_map/ppermute | solution.py:18
  55.3 1.6 %collective-permute-start.9 = (bf16[1,128,256]{2,1,0:T(8,128)(2,1)S(1)}, bf16[1,128,256]{2,1,0:T(8,128)(2,1)S(1)}, u32[]{:S(2)}, u32[]{:S(2)}) collective-permute-start(bf16[1,128,256]{2,1,0:T(8,128)(2,1)S(1)} %copy.173), channel_id=1, source_target_pairs={{0,2},{2,0},{4,6},{6,4},{8,10},{10,8},{12,14},{14,12},{1,3},{3,1},... | collective-permute-start | bytes 196616 | tf_op jit(solution)/shard_map/ppermute | solution.py:18
  56.9 0.4 mul.132
  57.3 0.7 mul.133
  58.0 2.6 %scatter_custom_fusion = bf16[320,1024]{1,0:T(8,128)(2,1)} fusion(s32[256]{0:T(256)S(1)} %bitcast.149, f32[256,1024]{1,0:T(8,128)S(1)} %mul.133, f32[256]{0:T(256)S(1)} %mul.130, bf16[]{:T(256)} %constant.112.clone.1), kind=kCustom, calls=%fused_computation.28 | custom fusion | flops 524288 | bytes 1704962 | tf_op jit(solution)/shard_map/scatter | solution.py:197
  60.6 3.5 %all-to-all-start.1 = ((bf16[1,4,1,80,1024]{4,3,2,0,1:T(8,128)(2,1)}), bf16[1,4,1,80,1024]{4,3,2,0,1:T(8,128)(2,1)S(1)}, u32[]{:S(2)}, u32[]{:S(2)}) async-start(bf16[1,4,1,80,1024]{4,3,2,0,1:T(8,128)(2,1)} %bitcast.43), calls=%async_computation.1 | async-start | bytes 1310720 | tf_op jit(solution)/shard_map/all_to_all | solution.py:199
  64.1 4.2 %convolution_convert_fusion = bf16[2,128,4,128]{3,1,2,0:T(8,128)(2,1)S(1)} fusion(bf16[512,2,128,1]{0,2,3,1:T(8,128)(2,1)S(1)} %bitcast.139, f32[2,512,128,4]{2,1,3,0:T(8,128)} %fusion.45, f32[2,4,128,512]{2,3,1,0:T(8,128)} %get-tuple-element.62, f32[2,4,128]{2,1,0:T(4,128)S(1)} %get-tuple-element.61), kind=kOutput, calls=%fused_computation.17 | convolution fusion | flops 138020352 | bytes 4722688 | tf_op jit(solution)/shard_map/kgqs,skd->qkgd/dot_general | solution.py:162
  68.3 4.2 %fusion.43 = (bf16[512,2,128]{0,2,1:T(8,128)(2,1)S(1)}, f32[512,2,128]{0,2,1:T(8,128)S(1)}) fusion(bf16[128,2,4,128]{0,3,2,1:T(8,128)(2,1)S(1)} %bitcast.137, f32[2,512,128,4]{2,1,3,0:T(8,128)} %fusion.45, f32[2,4,128,512]{2,3,1,0:T(8,128)} %get-tuple-element.62, f32[2,4,128]{2,1,0:T(4,128)S(1)} %get-tuple-element.61), kind=kOutput, calls=%fused_computation.83 | convolution fusion | flops 138020352 | bytes 5246976 | tf_op jit(solution)/shard_map/rcnw,nrco->wro/dot_general | solution.py:166
  72.6 0.9 %slice.99 = f32[128,2,128]{0,2,1:T(8,128)S(1)} slice(f32[512,2,128]{0,2,1:T(8,128)} %get-tuple-element.68), slice={[0:128], [0:2], [0:128]} | slice | bytes 262144 | tf_op jit(solution)/shard_map/slice | solution.py:170
  73.9 0.9 copy.178
  74.8 3.0 %collective-permute-start.7 = (bf16[1,128,256]{2,1,0:T(8,128)(2,1)S(1)}, bf16[1,128,256]{2,1,0:T(8,128)(2,1)S(1)}, u32[]{:S(2)}, u32[]{:S(2)}) collective-permute-start(bf16[1,128,256]{2,1,0:T(8,128)(2,1)S(1)} %copy.169), channel_id=1, source_target_pairs={{0,4},{2,6},{4,0},{6,2},{8,12},{10,14},{12,8},{14,10},{1,5},{3,7},... | collective-permute-start | bytes 196616 | tf_op jit(solution)/shard_map/ppermute | solution.py:18
  77.8 0.5 collective-permute-start.8
  78.4 1.5 %collective-permute-start.6 = (bf16[1,128,256]{2,1,0:T(8,128)(2,1)S(1)}, bf16[1,128,256]{2,1,0:T(8,128)(2,1)S(1)}, u32[]{:S(2)}, u32[]{:S(2)}) collective-permute-start(bf16[1,128,256]{2,1,0:T(8,128)(2,1)S(1)} %copy.167), channel_id=1, source_target_pairs={{0,2},{2,0},{4,6},{6,4},{8,10},{10,8},{12,14},{14,12},{1,3},{3,1},... | collective-permute-start | bytes 196616 | tf_op jit(solution)/shard_map/ppermute | solution.py:18
  80.0 0.7 add_bitcast_fusion
  80.7 3.5 %collective-permute-done.7 = bf16[1,128,256]{2,1,0:T(8,128)(2,1)S(1)} collective-permute-done((bf16[1,128,256]{2,1,0:T(8,128)(2,1)S(1)}, bf16[1,128,256]{2,1,0:T(8,128)(2,1)S(1)}, u32[]{:S(2)}, u32[]{:S(2)}) %collective-permute-start.7) | collective-permute-done | bytes 65568 | tf_op jit(solution)/shard_map/ppermute | solution.py:18
  84.2 0.6 collective-permute-done.6
  84.8 0.7 add_bitcast_fusion.1
  85.5 0.8 copy.198
  (70 shorter events, 3.9 us)
Async XLA Ops:
  0.6 39.3 %copy-start = (f32[1024,64]{0,1:T(8,128)S(1)}, f32[1024,64]{0,1:T(8,128)}, u32[]{:S(2)}) copy-start(f32[1024,64]{0,1:T(8,128)} %param.27) | copy-start | bytes 786436
  0.6 24.8 %copy-start.3 = (bf16[128,256]{1,0:T(8,128)(2,1)S(1)}, bf16[128,256]{1,0:T(8,128)(2,1)}, u32[]{:S(2)}) copy-start(bf16[128,256]{1,0:T(8,128)(2,1)} %param.18) | copy-start | bytes 196612
  0.7 22.2 %copy-start.4 = (s32[128,2]{0,1:T(2,128)S(1)}, s32[128,2]{0,1:T(2,128)}, u32[]{:S(2)}) copy-start(s32[128,2]{0,1:T(2,128)} %param.21) | copy-start | bytes 3076
  0.7 22.3 %copy-start.1 = (bf16[128,1024]{1,0:T(8,128)(2,1)S(1)}, bf16[128,1024]{1,0:T(8,128)(2,1)}, u32[]{:S(2)}) copy-start(bf16[128,1024]{1,0:T(8,128)(2,1)} %param.16) | copy-start | bytes 786436
  1.7 23.9 %collective-permute-start.2 = (bf16[128,256]{0,1:T(8,128)(2,1)S(1)}, bf16[128,256]{0,1:T(8,128)(2,1)S(1)}, u32[]{:S(2)}, u32[]{:S(2)}) collective-permute-start(bf16[128,256]{0,1:T(8,128)(2,1)S(1)} %copy.146), channel_id=1, source_target_pairs={{0,8},{2,10},{4,12},{6,14},{8,0},{10,2},{12,4},{14,6},{1,9},{3,11}... | collective-permute-start | bytes 196616 | tf_op jit(solution)/shard_map/ppermute | solution.py:18
  4.7 20.9 %collective-permute-start.1 = (bf16[128,256]{0,1:T(8,128)(2,1)S(1)}, bf16[128,256]{0,1:T(8,128)(2,1)S(1)}, u32[]{:S(2)}, u32[]{:S(2)}) collective-permute-start(bf16[128,256]{0,1:T(8,128)(2,1)S(1)} %copy.146), channel_id=1, source_target_pairs={{0,4},{2,6},{4,0},{6,2},{8,12},{10,14},{12,8},{14,10},{1,5},{3,7},... | collective-permute-start | bytes 196616 | tf_op jit(solution)/shard_map/ppermute | solution.py:18
  7.3 16.0 %collective-permute-start.4 = (bf16[128,256]{1,0:T(8,128)(2,1)}, bf16[128,256]{1,0:T(8,128)(2,1)S(1)}, u32[]{:S(2)}, u32[]{:S(2)}) collective-permute-start(bf16[128,256]{1,0:T(8,128)(2,1)} %param.18), channel_id=1, source_target_pairs={{0,4},{2,6},{4,0},{6,2},{8,12},{10,14},{12,8},{14,10},{1,5},{3,7},... | collective-permute-start | bytes 196616 | tf_op jit(solution)/shard_map/ppermute | solution.py:18
  7.6 17.8 %collective-permute-start.3 = (bf16[128,256]{1,0:T(8,128)(2,1)}, bf16[128,256]{1,0:T(8,128)(2,1)S(1)}, u32[]{:S(2)}, u32[]{:S(2)}) collective-permute-start(bf16[128,256]{1,0:T(8,128)(2,1)} %param.18), channel_id=1, source_target_pairs={{0,2},{2,0},{4,6},{6,4},{8,10},{10,8},{12,14},{14,12},{1,3},{3,1},... | collective-permute-start | bytes 196616 | tf_op jit(solution)/shard_map/ppermute | solution.py:18
  9.2 16.2 %collective-permute-start.5 = (bf16[128,256]{1,0:T(8,128)(2,1)}, bf16[128,256]{1,0:T(8,128)(2,1)S(1)}, u32[]{:S(2)}, u32[]{:S(2)}) collective-permute-start(bf16[128,256]{1,0:T(8,128)(2,1)} %param.18), channel_id=1, source_target_pairs={{0,8},{2,10},{4,12},{6,14},{8,0},{10,2},{12,4},{14,6},{1,9},{3,11}... | collective-permute-start | bytes 196616 | tf_op jit(solution)/shard_map/ppermute | solution.py:18
  9.7 24.4 %all-to-all-start = ((bf16[1,1,4,80,1024]{4,3,1,0,2:T(8,128)(2,1)}), bf16[1,1,4,80,1024]{4,3,1,0,2:T(8,128)(2,1)S(1)}, u32[]{:S(2)}, u32[]{:S(2)}) async-start(bf16[1,1,4,80,1024]{4,3,1,0,2:T(8,128)(2,1)} %bitcast.132), calls=%async_computation | async-start | bytes 1310720 | tf_op jit(solution)/shard_map/all_to_all | solution.py:111
  23.3 6.5 %collective-permute-start = (bf16[128,256]{0,1:T(8,128)(2,1)S(1)}, bf16[128,256]{0,1:T(8,128)(2,1)S(1)}, u32[]{:S(2)}, u32[]{:S(2)}) collective-permute-start(bf16[128,256]{0,1:T(8,128)(2,1)S(1)} %copy.146), channel_id=1, source_target_pairs={{0,2},{2,0},{4,6},{6,4},{8,10},{10,8},{12,14},{14,12},{1,3},{3,1},... | collective-permute-start | bytes 196616 | tf_op jit(solution)/shard_map/ppermute | solution.py:18
  35.3 1.9 %copy-start.2 = (bf16[128,1024]{1,0:T(8,128)(2,1)S(1)}, bf16[128,1024]{1,0:T(8,128)(2,1)}, u32[]{:S(2)}) copy-start(bf16[128,1024]{1,0:T(8,128)(2,1)} %param.19) | copy-start | bytes 786436
  35.3 4.6 %copy-start.5 = (f32[1024]{0:T(1024)S(1)}, f32[1024]{0:T(1024)}, u32[]{:S(2)}) copy-start(f32[1024]{0:T(1024)} %param.26) | copy-start | bytes 12292
  37.2 6.9 %copy-start.6 = (f32[64,64]{1,0:T(8,128)S(1)}, f32[64,64]{1,0:T(8,128)}, u32[]{:S(2)}) copy-start(f32[64,64]{1,0:T(8,128)} %param.25) | copy-start | bytes 49156
  52.9 25.5 %collective-permute-start.10 = (bf16[1,128,256]{2,1,0:T(8,128)(2,1)S(1)}, bf16[1,128,256]{2,1,0:T(8,128)(2,1)S(1)}, u32[]{:S(2)}, u32[]{:S(2)}) collective-permute-start(bf16[1,128,256]{2,1,0:T(8,128)(2,1)S(1)} %copy.175), channel_id=1, source_target_pairs={{0,4},{2,6},{4,0},{6,2},{8,12},{10,14},{12,8},{14,10},{1,5},{3,7},... | collective-permute-start | bytes 196616 | tf_op jit(solution)/shard_map/ppermute | solution.py:18
  53.8 26.2 %collective-permute-start.11 = (bf16[1,128,256]{2,1,0:T(8,128)(2,1)S(1)}, bf16[1,128,256]{2,1,0:T(8,128)(2,1)S(1)}, u32[]{:S(2)}, u32[]{:S(2)}) collective-permute-start(bf16[1,128,256]{2,1,0:T(8,128)(2,1)S(1)} %copy.176), channel_id=1, source_target_pairs={{0,8},{2,10},{4,12},{6,14},{8,0},{10,2},{12,4},{14,6},{1,9},{3,11}... | collective-permute-start | bytes 196616 | tf_op jit(solution)/shard_map/ppermute | solution.py:18
  55.3 24.7 %collective-permute-start.9 = (bf16[1,128,256]{2,1,0:T(8,128)(2,1)S(1)}, bf16[1,128,256]{2,1,0:T(8,128)(2,1)S(1)}, u32[]{:S(2)}, u32[]{:S(2)}) collective-permute-start(bf16[1,128,256]{2,1,0:T(8,128)(2,1)S(1)} %copy.173), channel_id=1, source_target_pairs={{0,2},{2,0},{4,6},{6,4},{8,10},{10,8},{12,14},{14,12},{1,3},{3,1},... | collective-permute-start | bytes 196616 | tf_op jit(solution)/shard_map/ppermute | solution.py:18
  60.6 24.9 %all-to-all-start.1 = ((bf16[1,4,1,80,1024]{4,3,2,0,1:T(8,128)(2,1)}), bf16[1,4,1,80,1024]{4,3,2,0,1:T(8,128)(2,1)S(1)}, u32[]{:S(2)}, u32[]{:S(2)}) async-start(bf16[1,4,1,80,1024]{4,3,2,0,1:T(8,128)(2,1)} %bitcast.43), calls=%async_computation.1 | async-start | bytes 1310720 | tf_op jit(solution)/shard_map/all_to_all | solution.py:199
  74.8 9.4 %collective-permute-start.7 = (bf16[1,128,256]{2,1,0:T(8,128)(2,1)S(1)}, bf16[1,128,256]{2,1,0:T(8,128)(2,1)S(1)}, u32[]{:S(2)}, u32[]{:S(2)}) collective-permute-start(bf16[1,128,256]{2,1,0:T(8,128)(2,1)S(1)} %copy.169), channel_id=1, source_target_pairs={{0,4},{2,6},{4,0},{6,2},{8,12},{10,14},{12,8},{14,10},{1,5},{3,7},... | collective-permute-start | bytes 196616 | tf_op jit(solution)/shard_map/ppermute | solution.py:18
  77.8 6.4 %collective-permute-start.8 = (bf16[1,128,256]{2,1,0:T(8,128)(2,1)S(1)}, bf16[1,128,256]{2,1,0:T(8,128)(2,1)S(1)}, u32[]{:S(2)}, u32[]{:S(2)}) collective-permute-start(bf16[1,128,256]{2,1,0:T(8,128)(2,1)S(1)} %copy.170), channel_id=1, source_target_pairs={{0,8},{2,10},{4,12},{6,14},{8,0},{10,2},{12,4},{14,6},{1,9},{3,11}... | collective-permute-start | bytes 196616 | tf_op jit(solution)/shard_map/ppermute | solution.py:18
  78.4 6.4 %collective-permute-start.6 = (bf16[1,128,256]{2,1,0:T(8,128)(2,1)S(1)}, bf16[1,128,256]{2,1,0:T(8,128)(2,1)S(1)}, u32[]{:S(2)}, u32[]{:S(2)}) collective-permute-start(bf16[1,128,256]{2,1,0:T(8,128)(2,1)S(1)} %copy.167), channel_id=1, source_target_pairs={{0,2},{2,0},{4,6},{6,4},{8,10},{10,8},{12,14},{14,12},{1,3},{3,1},... | collective-permute-start | bytes 196616 | tf_op jit(solution)/shard_map/ppermute | solution.py:18
where the time goes:
time: 86.8 us; the launch traced here: 86.3 us
  starting transfers between devices  26.5 us (31%)
  matrix products  18.9 us (22%)
  local copies, waits for them, and re-layouts  12.7 us (15%)
  other arithmetic  10.4 us (12%)
  waiting for transfers between devices  8.35 us (10%)
  blocking collectives  8.33 us (10%)
  between operations  1.07 us (1%)
    ppermute x12, starting transfers between devices, swapped(): lax.ppermute(array, axis, [(i, i ^ 1 << distance) for i in range(lax.axis...  19.1 us
    ppermute x12, waiting for transfers between devices, swapped(): lax.ppermute(array, axis, [(i, i ^ 1 << distance) for i in range(lax.axis...  8.34 us
    unnamed x19, local copies, waits for them, and re-layouts  4.31 us
    dot_general x1, matrix products, local(): jnp.einsum('rcnw,nrco->wro', grad_score, q_blocks[block_position], prefer...  4.24 us
    dot_general x1, matrix products, local(): jnp.einsum('kgqs,skd->qkgd', grad_score, key_set, preferred_element_type=...  4.23 us
    all_to_all x1, starting transfers between devices, local(): lax.all_to_all(expert_out, 'expert', split_axis=2, concat_axis=1, tiled=T...  3.86 us
    all_to_all x1, starting transfers between devices, local(): lax.all_to_all(buffer.reshape(1, experts, 1, capacity, -1), 'expert', spl...  3.48 us
    psum x1, blocking collectives, local(): lax.psum(jnp.dot(normed, head_weight, precision=HIGHEST_PRECISION), 'tens...  3.4 us
  transfers between devices with their start and end apart: 14, of which 3 were waited for; matrix products, arithmetic and copies ran while one was open for 35% of the time, Pallas kernels for 0%

commit v1 on v0

v1 whole, which is shorter than its diff:
```python
import functools

import jax
import jax.numpy as jnp
from jax import lax
from jax.experimental import pallas as pl
from jax.experimental.pallas import tpu as pltpu
from jax.sharding import PartitionSpec as P

BLOCK = 128
HEAD = 128
LOSS_SCALE = 256
D = 2048
EPSILON = 1e-05
NEGATIVE = -1e30
LOG2E = 1.4426950408889634
MESH = pl.DeviceIdType.MESH
NT = (((1,), (1,)), ((), ()))
NN = (((1,), (0,)), ((), ()))
TN = (((0,), (0,)), ((), ()))


def dot(a, b, dims):
    return lax.dot_general(a, b, dims, preferred_element_type=jnp.float32)


def flipped(index, bit):
    step = 1 << bit
    return index + step * (1 - 2 * ((index // step) % 2))


def body(
    n_context,
    n_expert,
    q_hbm,
    k_hbm,
    v_hbm,
    r_hbm,
    x_hbm,
    routes_hbm,
    rw_hbm,
    pat_hbm,
    len_hbm,
    tea_hbm,
    gain_hbm,
    hw_hbm,
    gq_v,
    gk_v,
    gv_v,
    gx_hbm,
    q_v,
    r_v,
    kbuf,
    vbuf,
    xbuf,
    routes_v,
    rw_v,
    pat_s,
    len_v,
    tea_v,
    gain_v,
    hw_v,
    qst,
    pt_v,
    ptb_v,
    attn_v,
    hid_v,
    dost,
    hw3_v,
    ex_send,
    ex_recv,
    gsend,
    grecv,
    xsend,
    in_sem,
    kv_send_sem,
    kv_recv_sem,
    x_send_sem,
    x_recv_sem,
    ex_sem,
    g_send_sem,
    g_recv_sem,
    gx_send_sem,
    gx_recv_sem,
):
    ctx = lax.axis_index("context")
    exp = lax.axis_index("expert")
    ten = lax.axis_index("tensor")
    shard = ctx * n_expert + exp
    e_bits = n_expert.bit_length() - 1
    c_bits = n_context.bit_length() - 1
    bits = e_bits + c_bits
    rows = q_v.shape[0]
    width = q_v.shape[1]
    kv_dev = kbuf.shape[2] // HEAD
    group = width // HEAD // kv_dev
    cap = xbuf.shape[1]
    span = (1 + bits) * BLOCK
    cats = hw_v.shape[0]
    turns = tea_v.shape[0]
    scale = HEAD ** (-0.5)

    def partner(bit):
        if bit < e_bits:
            return {"expert": flipped(exp, bit)}
        return {"context": flipped(ctx, bit - e_bits)}

    others = [{"expert": lax.rem(exp + off, n_expert)} for off in range(1, n_expert)]
    peers = others + [partner(bit) for bit in range(e_bits, bits)] + [{"tensor": 1 - ten}]
    barrier = pltpu.get_barrier_semaphore()
    for peer in peers:
        pl.semaphore_signal(barrier, inc=1, device_id=peer, device_id_type=MESH)

    local_list = [
        (q_hbm, q_v),
        (k_hbm, kbuf.at[0]),
        (v_hbm, vbuf.at[0]),
        (r_hbm, r_v),
        (x_hbm.at[0, 0, exp], xbuf.at[exp]),
        (routes_hbm, routes_v),
        (rw_hbm, rw_v),
        (pat_hbm, pat_s),
        (len_hbm, len_v),
        (tea_hbm, tea_v),
        (gain_hbm, gain_v),
        (hw_hbm, hw_v),
    ]
    local = [
        pltpu.make_async_copy(src, dst, in_sem.at[i]) for i, (src, dst) in enumerate(local_list)
    ]
    for copy in local:
        copy.start()
    pl.semaphore_wait(barrier, len(peers))

    kv_copies = []
    for bit in range(bits):
        for j, (src, dst) in enumerate(((k_hbm, kbuf), (v_hbm, vbuf))):
            copy = pltpu.make_async_remote_copy(
                src_ref=src,
                dst_ref=dst.at[1 + bit],
                send_sem=kv_send_sem.at[2 * bit + j],
                recv_sem=kv_recv_sem.at[2 * bit + j],
                device_id=partner(bit),
                device_id_type=MESH,
            )
            copy.start()
            kv_copies.append(copy)
    x_copies = []
    for off in range(1, n_expert):
        copy = pltpu.make_async_remote_copy(
            src_ref=x_hbm.at[0, 0, lax.rem(exp + off, n_expert)],
            dst_ref=xbuf.at[exp],
            send_sem=x_send_sem.at[off],
            recv_sem=x_recv_sem.at[off],
            device_id=others[off - 1],
            device_id_type=MESH,
        )
        copy.start()
        x_copies.append(copy)
    for copy in local:
        copy.wait()

    lane = lax.broadcasted_iota(jnp.int32, (rows, 128), 1)
    name = lax.broadcasted_iota(jnp.int32, (128, rows), 0)
    row = lax.broadcasted_iota(jnp.int32, (rows, rows), 0)
    col = lax.broadcasted_iota(jnp.int32, (rows, rows), 1)
    member = jnp.zeros((128, rows), jnp.float32)
    weight = jnp.zeros((128, rows), jnp.float32)
    for k in range(routes_v.shape[0]):
        hit = routes_v[k : k + 1, :] == name
        member = member + jnp.where(hit, 1.0, 0.0)
        weight = weight + jnp.where(hit, rw_v[k : k + 1, :], 0.0)
    before = dot(
        member.astype(jnp.bfloat16), jnp.where(row < col, 1.0, 0.0).astype(jnp.bfloat16), NN
    )
    slot = jnp.where(member > 0, before, -1.0).T
    weight = weight.T
    cap_lane = lax.broadcasted_iota(jnp.int32, (rows, cap), 1).astype(jnp.float32)

    def expert_pick(index):
        mine = lane == index
        slot_col = jnp.sum(jnp.where(mine, slot, 0.0), axis=1, keepdims=True)
        weight_col = jnp.sum(jnp.where(mine, weight, 0.0), axis=1, keepdims=True)
        onehot = jnp.where(slot_col == cap_lane, 1.0, 0.0).astype(jnp.bfloat16)
        return onehot, weight_col

    turn_row = lax.broadcasted_iota(jnp.int32, (turns, turns), 0)
    turn_col = lax.broadcasted_iota(jnp.int32, (turns, turns), 1)
    length_row = len_v[...].astype(jnp.float32)
    ends = jnp.sum(jnp.where(turn_col <= turn_row, length_row, 0.0), axis=1, keepdims=True)
    starts = jnp.sum(jnp.where(turn_col < turn_row, length_row, 0.0), axis=1, keepdims=True)
    position = (
        lax.broadcasted_iota(jnp.int32, (turns, rows), 1) + shard * rows
    ).astype(jnp.float32)
    turn_pick = jnp.where((starts <= position) & (position < ends), 1.0, 0.0)
    target = lax.dot_general(
        turn_pick,
        tea_v[...],
        TN,
        precision=lax.Precision.HIGHEST,
        preferred_element_type=jnp.float32,
    )

    hw = hw_v[...]
    hw_hi = hw.astype(jnp.bfloat16)
    hw_lo = (hw - hw_hi.astype(jnp.float32)).astype(jnp.bfloat16)
    hw3_v[...] = jnp.concatenate([hw_hi, hw_lo, hw_hi], axis=0)

    for g in range(kv_dev):
        for h in range(group):
            head = g * group + h
            qst[g, h * rows : (h + 1) * rows, :] = q_v[:, head * HEAD : (head + 1) * HEAD]

    for copy in kv_copies:
        copy.wait_recv()
    keep = [jnp.float32(1.0)]
    for bit in range(bits):
        other = flipped(exp, bit) + ctx * n_expert
        if bit >= e_bits:
            other = flipped(ctx, bit - e_bits) * n_expert + exp
        keep.append(pat_s[0, other].astype(jnp.float32))
    for g in range(kv_dev):
        lanes = slice(g * HEAD, (g + 1) * HEAD)
        parts = []
        for b in range(1 + bits):
            s = dot(kbuf[b, :, lanes], qst[g], NT)
            if b == 0:
                parts.append(s * (scale * LOG2E))
            else:
                parts.append(s * (keep[b] * (scale * LOG2E)) + (1.0 - keep[b]) * NEGATIVE)
        top_score = functools.reduce(
            jnp.maximum, [jnp.max(s, axis=0, keepdims=True) for s in parts]
        )
        parts = [jnp.exp2(s - top_score) for s in parts]
        total = functools.reduce(jnp.add, [jnp.sum(s, axis=0, keepdims=True) for s in parts])
        inverse = 1.0 / total
        for b in range(1 + bits):
            prob = parts[b] * inverse
            pt_v[g, b * BLOCK : (b + 1) * BLOCK, :] = prob
            ptb_v[g, b * BLOCK : (b + 1) * BLOCK, :] = prob.astype(jnp.bfloat16)
        value_set = vbuf[:, :, lanes].reshape(span, HEAD)
        out_t = dot(value_set, ptb_v[g], TN)
        for h in range(group):
            head = g * group + h
            attn_v[:, head * HEAD : (head + 1) * HEAD] = out_t[:, h * rows : (h + 1) * rows].T

    hid_v[...] = r_v[...].astype(jnp.float32) + attn_v[...]
    for off in range(n_expert):
        source = lax.rem(exp - off + n_expert, n_expert)
        if off:
            pltpu.make_async_copy(xbuf.at[source], xbuf.at[source], x_recv_sem.at[off]).wait()
        onehot, weight_col = expert_pick(source)
        hid_v[...] += weight_col * dot(onehot, xbuf[source], NN)

    hidden = hid_v[...]
    gain = gain_v[...]
    square = jnp.sum(hidden * hidden, axis=1, keepdims=True)
    scaled = hidden * gain
    part_hi = scaled.astype(jnp.bfloat16)
    part_lo = (scaled - part_hi.astype(jnp.float32)).astype(jnp.bfloat16)
    first = dot(part_hi, hw3_v[: 2 * cats, :], NT)
    raw_part = first[:, :cats] + first[:, cats:] + dot(part_lo, hw3_v[:cats, :], NT)
    ex_send[...] = jnp.concatenate([raw_part, jnp.broadcast_to(square, (rows, 128 - cats))], axis=1)
    ex_copy = pltpu.make_async_remote_copy(
        src_ref=ex_send,
        dst_ref=ex_recv,
        send_sem=ex_sem.at[0],
        recv_sem=ex_sem.at[1],
        device_id={"tensor": 1 - ten},
        device_id_type=MESH,
    )
    ex_copy.start()
    ex_copy.wait()
    both = ex_send[...] + ex_recv[...]
    raw = both[:, :cats]
    rms = jnp.sqrt(both[:, cats : cats + 1] / D + EPSILON)
    inv = 1.0 / rms
    grad_logit = (jax.nn.sigmoid(raw * inv) - target) * LOSS_SCALE
    inner = jnp.sum(grad_logit * raw, axis=1, keepdims=True)
    gl_hi = grad_logit.astype(jnp.bfloat16)
    gl_lo = (grad_logit - gl_hi.astype(jnp.float32)).astype(jnp.bfloat16)
    normed = dot(jnp.concatenate([gl_hi, gl_hi, gl_lo], axis=1), hw3_v[...], NN)
    grad_hidden = gain * normed * inv - hidden * (inner / (D * rms * rms * rms))
    hid_v[...] = grad_hidden

    gx_copies = []
    for off in list(range(1, n_expert)) + [0]:
        owner = lax.rem(exp + off, n_expert)
        onehot, weight_col = expert_pick(owner)
        weighted = (weight_col * hid_v[...]).astype(jnp.bfloat16)
        xsend[off] = dot(onehot, weighted, TN).astype(jnp.bfloat16)
        if off:
            copy = pltpu.make_async_remote_copy(
                src_ref=xsend.at[off],
                dst_ref=gx_hbm.at[0, 0, exp],
                send_sem=gx_send_sem.at[off],
                recv_sem=gx_recv_sem.at[off],
                device_id=others[off - 1],
                device_id_type=MESH,
            )
        else:
            copy = pltpu.make_async_copy(xsend.at[0], gx_hbm.at[0, 0, exp], gx_send_sem.at[0])
        copy.start()
        gx_copies.append(copy)

    for g in range(kv_dev):
        for h in range(group):
            head = g * group + h
            dost[g, h * rows : (h + 1) * rows, :] = hid_v[
                :, head * HEAD : (head + 1) * HEAD
            ].astype(jnp.bfloat16)
    for g in range(kv_dev):
        lanes = slice(g * HEAD, (g + 1) * HEAD)
        key_set = kbuf[:, :, lanes].reshape(span, HEAD)
        value_set = vbuf[:, :, lanes].reshape(span, HEAD)
        grad_prob = dot(value_set, dost[g], NT)
        prob = pt_v[g]
        delta = jnp.sum(prob * grad_prob, axis=0, keepdims=True)
        score = (prob * (grad_prob - delta) * scale).astype(jnp.bfloat16)
        key_grad = dot(score, qst[g], NN)
        value_grad = dot(ptb_v[g], dost[g], NN)
        gk_v[:, lanes] = key_grad[:BLOCK]
        gv_v[:, lanes] = value_grad[:BLOCK]
        for b in range(bits):
            rows_b = slice((1 + b) * BLOCK, (2 + b) * BLOCK)
            gsend[b, 0, :, lanes] = key_grad[rows_b].astype(jnp.bfloat16)
            gsend[b, 1, :, lanes] = value_grad[rows_b].astype(jnp.bfloat16)
        query_t = dot(key_set, score, TN)
        for h in range(group):
            head = g * group + h
            gq_v[:, head * HEAD : (head + 1) * HEAD] = query_t[:, h * rows : (h + 1) * rows].T.astype(
                jnp.bfloat16
            )
    g_copies = []
    for bit in range(bits):
        copy = pltpu.make_async_remote_copy(
            src_ref=gsend.at[bit],
            dst_ref=grecv.at[bit],
            send_sem=g_send_sem.at[bit],
            recv_sem=g_recv_sem.at[bit],
            device_id=partner(bit),
            device_id_type=MESH,
        )
        copy.start()
        g_copies.append(copy)
    for bit in range(bits):
        g_copies[bit].wait_recv()
        gk_v[...] += grecv[bit, 0].astype(jnp.float32)
        gv_v[...] += grecv[bit, 1].astype(jnp.float32)
    for copy in kv_copies + x_copies + g_copies:
        copy.wait_send()
    for copy in gx_copies:
        copy.wait()


def solution(mesh):
    n_context = mesh.shape["context"]
    n_expert = mesh.shape["expert"]
    bits = (n_context * n_expert).bit_length() - 1

    def local(
        queries,
        keys,
        values,
        resid,
        expert_out,
        routes,
        route_weights,
        pattern,
        lengths,
        teacher,
        gain,
        head_weight,
    ):
        rows, width = queries.shape
        kv_width = keys.shape[1]
        kv_dev = kv_width // HEAD
        group = width // HEAD // kv_dev
        span = (1 + bits) * BLOCK
        cap = expert_out.shape[3]
        lengths = lengths.reshape(1, -1)
        gain = gain.reshape(1, -1)
        cats = head_weight.shape[1]
        head_weight, routes, route_weights = head_weight.T, routes.T, route_weights.T
        bf16, f32 = jnp.bfloat16, jnp.float32
        dma = pltpu.SemaphoreType.DMA
        args = (
            queries,
            keys,
            values,
            resid,
            expert_out,
            routes,
            route_weights,
            pattern,
            lengths,
            teacher,
            gain,
            head_weight,
        )
        scratch = [
            pltpu.VMEM((rows, width), bf16),
            pltpu.VMEM((rows, width), bf16),
            pltpu.VMEM((1 + bits, rows, kv_width), bf16),
            pltpu.VMEM((1 + bits, rows, kv_width), bf16),
            pltpu.VMEM((n_expert, cap, width), bf16),
            pltpu.VMEM(routes.shape, jnp.int32),
            pltpu.VMEM(route_weights.shape, f32),
            pltpu.SMEM(pattern.shape, jnp.int32),
            pltpu.VMEM(lengths.shape, jnp.int32),
            pltpu.VMEM(teacher.shape, f32),
            pltpu.VMEM(gain.shape, f32),
            pltpu.VMEM(head_weight.shape, f32),
            pltpu.VMEM((kv_dev, group * rows, HEAD), bf16),
            pltpu.VMEM((kv_dev, span, group * rows), f32),
            pltpu.VMEM((kv_dev, span, group * rows), bf16),
            pltpu.VMEM((rows, width), f32),
            pltpu.VMEM((rows, width), f32),
            pltpu.VMEM((kv_dev, group * rows, HEAD), bf16),
            pltpu.VMEM((3 * cats, width), bf16),
            pltpu.VMEM((rows, 128), f32),
            pltpu.VMEM((rows, 128), f32),
            pltpu.VMEM((bits, 2, rows, kv_width), bf16),
            pltpu.VMEM((bits, 2, rows, kv_width), bf16),
            pltpu.VMEM((n_expert, cap, width), bf16),
            dma((len(args),)),
            dma((2 * bits,)),
            dma((2 * bits,)),
            dma((n_expert,)),
            dma((n_expert,)),
            dma((2,)),
            dma((bits,)),
            dma((bits,)),
            dma((n_expert,)),
            dma((n_expert,)),
        ]
        return pl.pallas_call(
            functools.partial(body, n_context, n_expert),
            out_shape=(
                jax.ShapeDtypeStruct((rows, width), bf16),
                jax.ShapeDtypeStruct((rows, kv_width), f32),
                jax.ShapeDtypeStruct((rows, kv_width), f32),
                jax.ShapeDtypeStruct(expert_out.shape, bf16),
            ),
            in_specs=[pl.BlockSpec(memory_space=pltpu.HBM)] * len(args),
            out_specs=(pl.BlockSpec(memory_space=pltpu.VMEM),) * 4,
            scratch_shapes=scratch,
            compiler_params=pltpu.CompilerParams(
                collective_id=0, has_side_effects=True, vmem_limit_bytes=48 * 1024 * 1024
            ),
        )(*args)

    rows_spec = P(("groups", "context", "expert"), "tensor")
    expert_spec = P(("groups", "context"), "expert", None, None, "tensor")
    return jax.shard_map(
        local,
        mesh=mesh,
        in_specs=(
            rows_spec,
            rows_spec,
            rows_spec,
            rows_spec,
            expert_spec,
            P(("groups", "context", "expert"), None),
            P(("groups", "context", "expert"), None),
            P(("context", "expert"), None),
            P("groups"),
            P("groups", None),
            P("tensor"),
            P("tensor", None),
        ),
        out_specs=(rows_spec, rows_spec, rows_spec, expert_spec),
        check_vma=False,
    )
```

time: 86.8 us -> 60 us (0.69)
  Pallas kernels: 0 us -> 49 us
  starting transfers between devices: 26.5 us -> 0 us
  matrix products: 18.9 us -> 0 us
  other arithmetic: 10.4 us -> 0 us
  waiting for transfers between devices: 8.35 us -> 0 us
  blocking collectives: 8.33 us -> 0 us
  local copies, waits for them, and re-layouts: 12.7 us -> 9.91 us
    pallas_call x0 -> x1, Pallas kernels: none -> 49 us  [local(): pl.pallas_call(functools.partial(body, n_context, n_expert), out_shape=(j...]
    ppermute x12 -> x0, starting transfers between devices: 19.1 us -> none  [swapped(): lax.ppermute(array, axis, [(i, i ^ 1 << distance) for i in range(lax.axis...]
    dot_general x8 -> x0, matrix products: 16.7 us -> none  [the longest x1 4.24 us: local(): jnp.einsum('rcnw,nrco->wro', grad_score, q_blocks[block_position], prefer...]
    ppermute x12 -> x0, waiting for transfers between devices: 8.34 us -> none  [swapped(): lax.ppermute(array, axis, [(i, i ^ 1 << distance) for i in range(lax.axis...]
    psum x3 -> x0, blocking collectives: 8.33 us -> none  [the longest x1 3.4 us: local(): lax.psum(jnp.dot(normed, head_weight, precision=HIGHEST_PRECISION), 'tens...]
    all_to_all x2 -> x0, starting transfers between devices: 7.34 us -> none  [the longest x1 3.86 us: local(): lax.all_to_all(expert_out, 'expert', split_axis=2, concat_axis=1, tiled=T...]
    unnamed x19 -> x28, local copies, waits for them, and re-layouts: 4.31 us -> 9.91 us
    scatter x1 -> x0, other arithmetic: 2.59 us -> none  [local(): buffer = jnp.zeros((experts * capacity, grad_hidden.shape[1]), jnp.bfloat...]
  transfers between devices with their start and end apart: 14 -> 0, of which waited for: 3 -> 0; matrix products, arithmetic and copies ran while one was open for 35% -> 0% of each run, Pallas kernels for 0% -> 0%
where the time goes in v1:
time: 60 us; the launch traced here: 59.6 us
  Pallas kernels  49 us (82%)
  local copies, waits for them, and re-layouts  9.91 us (17%)
  between operations  0.69 us (1%)
    pallas_call x1, Pallas kernels, local(): pl.pallas_call(functools.partial(body, n_context, n_expert), out_shape=(j...  49 us
    unnamed x28, local copies, waits for them, and re-layouts  9.91 us

profile of v1, /device:TPU:0, one launch (start us, length us, event | category | flops | bytes accessed | tf_op | source)
XLA Modules:
  0.0 59.6 jit_solution(15437922880756712322)
XLA Ops:
  0.6 0.0 copy-start.7
  0.6 0.0 copy-start.9
  0.7 0.0 copy-start.11
  0.7 0.0 copy-start.8
  0.7 0.0 copy-start.10
  0.7 0.6 %copy-done.7 = f32[1024]{0:T(1024)S(1)} copy-done((f32[1024]{0:T(1024)S(1)}, f32[1024]{0:T(1024)}, u32[]{:S(2)}) %copy-start.7) | copy-done | bytes 4120
  1.3 0.0 copy-done.9
  1.3 0.0 copy-done.11
  1.3 0.0 copy-done.8
  1.4 0.0 copy-done.10
  1.4 0.0 copy-start
  1.4 1.1 %copy-done = bf16[1,1,4,80,1024]{4,3,2,1,0:T(8,128)(2,1)S(1)} copy-done((bf16[1,1,4,80,1024]{4,3,2,1,0:T(8,128)(2,1)S(1)}, bf16[1,1,4,80,1024]{4,3,2,1,0:T(8,128)(2,1)}, u32[]{:S(2)}) %copy-start) | copy-done | bytes 655384
  2.5 0.0 copy-start.1
  2.5 0.9 %copy-done.1 = bf16[128,1024]{1,0:T(8,128)(2,1)S(1)} copy-done((bf16[128,1024]{1,0:T(8,128)(2,1)S(1)}, bf16[128,1024]{1,0:T(8,128)(2,1)}, u32[]{:S(2)}) %copy-start.1) | copy-done | bytes 262168
  3.4 0.0 copy-start.2
  3.4 0.9 %copy-done.2 = bf16[128,1024]{1,0:T(8,128)(2,1)S(1)} copy-done((bf16[128,1024]{1,0:T(8,128)(2,1)S(1)}, bf16[128,1024]{1,0:T(8,128)(2,1)}, u32[]{:S(2)}) %copy-start.2) | copy-done | bytes 262168
  4.4 0.0 copy-start.3
  4.4 0.9 %copy-done.3 = f32[1024,64]{0,1:T(8,128)S(1)} copy-done((f32[1024,64]{0,1:T(8,128)S(1)}, f32[1024,64]{0,1:T(8,128)}, u32[]{:S(2)}) %copy-start.3) | copy-done | bytes 262168
  5.3 0.0 copy-start.4
  5.3 0.8 %copy-done.4 = bf16[128,256]{1,0:T(8,128)(2,1)S(1)} copy-done((bf16[128,256]{1,0:T(8,128)(2,1)S(1)}, bf16[128,256]{1,0:T(8,128)(2,1)}, u32[]{:S(2)}) %copy-start.4) | copy-done | bytes 65560
  6.1 0.0 copy-start.5
  6.1 0.8 %copy-done.5 = bf16[128,256]{1,0:T(8,128)(2,1)S(1)} copy-done((bf16[128,256]{1,0:T(8,128)(2,1)S(1)}, bf16[128,256]{1,0:T(8,128)(2,1)}, u32[]{:S(2)}) %copy-start.5) | copy-done | bytes 65560
  7.0 0.0 copy-start.6
  7.0 0.8 %copy-done.6 = f32[64,64]{1,0:T(8,128)S(1)} copy-done((f32[64,64]{1,0:T(8,128)S(1)}, f32[64,64]{1,0:T(8,128)}, u32[]{:S(2)}) %copy-start.6) | copy-done | bytes 16408
  7.7 49.0 %shard_map.147 = (bf16[128,1024]{1,0:T(8,128)(2,1)S(1)}, f32[128,256]{1,0:T(8,128)S(1)}, f32[128,256]{1,0:T(8,128)S(1)}, bf16[1,1,4,80,1024]{4,3,2,1,0:T(8,128)(2,1)S(1)}) custom-call(bf16[128,1024]{1,0:T(8,128)(2,1)S(1)} %copy-done.1, bf16[128,256]{1,0:T(8,128)(2,1)S(1)} %copy-done.4, bf16[128,256]{1,0:T(8,128)(2,1)S(1)} %copy-done.5, ...), custom_call_target="tpu_custom_call" | custom-call | tf_op jit(solution)/shard_map/pallas_call | solution.py:437
  56.7 0.7 %copy.20 = bf16[128,1024]{1,0:T(8,128)(2,1)} copy(bf16[128,1024]{1,0:T(8,128)(2,1)S(1)} %get-tuple-element.8) | data formatting | bytes 524288
  57.4 0.7 %copy.21 = f32[128,256]{1,0:T(8,128)} copy(f32[128,256]{1,0:T(8,128)S(1)} %get-tuple-element.9) | data formatting | bytes 262144
  58.1 0.7 %copy.22 = f32[128,256]{1,0:T(8,128)} copy(f32[128,256]{1,0:T(8,128)S(1)} %get-tuple-element.10) | data formatting | bytes 262144
  58.8 0.8 %copy.23 = bf16[1,1,4,80,1024]{4,3,2,1,0:T(8,128)(2,1)} copy(bf16[1,1,4,80,1024]{4,3,2,1,0:T(8,128)(2,1)S(1)} %get-tuple-element.11) | data formatting | bytes 1310720
Async XLA Ops:
  0.6 0.7 %copy-start.7 = (f32[1024]{0:T(1024)S(1)}, f32[1024]{0:T(1024)}, u32[]{:S(2)}) copy-start(f32[1024]{0:T(1024)} %param.22) | copy-start | bytes 12292
  0.6 0.7 %copy-start.9 = (f32[128,2]{0,1:T(2,128)S(1)}, f32[128,2]{0,1:T(2,128)}, u32[]{:S(2)}) copy-start(f32[128,2]{0,1:T(2,128)} %param.18) | copy-start | bytes 3076
  0.7 0.7 %copy-start.11 = (s32[64]{0:T(128)S(1)}, s32[64]{0:T(128)}, u32[]{:S(2)}) copy-start(s32[64]{0:T(128)} %param.20) | copy-start | bytes 772
  0.7 0.7 %copy-start.8 = (s32[128,2]{0,1:T(2,128)S(1)}, s32[128,2]{0,1:T(2,128)}, u32[]{:S(2)}) copy-start(s32[128,2]{0,1:T(2,128)} %param.17) | copy-start | bytes 3076
  0.7 0.7 %copy-start.10 = (s32[1,8]{1,0:T(1,128)S(1)}, s32[1,8]{1,0:T(1,128)}, u32[]{:S(2)}) copy-start(s32[1,8]{1,0:T(1,128)} %pat_hbm.1) | copy-start | bytes 100
  1.4 1.1 %copy-start = (bf16[1,1,4,80,1024]{4,3,2,1,0:T(8,128)(2,1)S(1)}, bf16[1,1,4,80,1024]{4,3,2,1,0:T(8,128)(2,1)}, u32[]{:S(2)}) copy-start(bf16[1,1,4,80,1024]{4,3,2,1,0:T(8,128)(2,1)} %x_hbm.1) | copy-start | bytes 1966084
  2.5 0.9 %copy-start.1 = (bf16[128,1024]{1,0:T(8,128)(2,1)S(1)}, bf16[128,1024]{1,0:T(8,128)(2,1)}, u32[]{:S(2)}) copy-start(bf16[128,1024]{1,0:T(8,128)(2,1)} %q_hbm.1) | copy-start | bytes 786436
  3.4 0.9 %copy-start.2 = (bf16[128,1024]{1,0:T(8,128)(2,1)S(1)}, bf16[128,1024]{1,0:T(8,128)(2,1)}, u32[]{:S(2)}) copy-start(bf16[128,1024]{1,0:T(8,128)(2,1)} %r_hbm.1) | copy-start | bytes 786436
  4.4 0.9 %copy-start.3 = (f32[1024,64]{0,1:T(8,128)S(1)}, f32[1024,64]{0,1:T(8,128)}, u32[]{:S(2)}) copy-start(f32[1024,64]{0,1:T(8,128)} %param.23) | copy-start | bytes 786436
  5.3 0.8 %copy-start.4 = (bf16[128,256]{1,0:T(8,128)(2,1)S(1)}, bf16[128,256]{1,0:T(8,128)(2,1)}, u32[]{:S(2)}) copy-start(bf16[128,256]{1,0:T(8,128)(2,1)} %k_hbm.1) | copy-start | bytes 196612
  6.1 0.8 %copy-start.5 = (bf16[128,256]{1,0:T(8,128)(2,1)S(1)}, bf16[128,256]{1,0:T(8,128)(2,1)}, u32[]{:S(2)}) copy-start(bf16[128,256]{1,0:T(8,128)(2,1)} %v_hbm.1) | copy-start | bytes 196612
  7.0 0.8 %copy-start.6 = (f32[64,64]{1,0:T(8,128)S(1)}, f32[64,64]{1,0:T(8,128)}, u32[]{:S(2)}) copy-start(f32[64,64]{1,0:T(8,128)} %tea_hbm.1) | copy-start | bytes 49156

commit v2 on v1

--- a/solution.py
+++ b/solution.py
@@ -44,9 +44,9 @@
     tea_hbm,
     gain_hbm,
     hw_hbm,
-    gq_v,
-    gk_v,
-    gv_v,
+    gq_hbm,
+    gk_hbm,
+    gv_hbm,
     gx_hbm,
     q_v,
     r_v,
@@ -72,6 +72,9 @@
     gsend,
     grecv,
     xsend,
+    gq_v,
+    gk_v,
+    gv_v,
     in_sem,
     kv_send_sem,
     kv_recv_sem,
@@ -82,6 +85,7 @@
     g_recv_sem,
     gx_send_sem,
     gx_recv_sem,
+    out_sem,
 ):
     ctx = lax.axis_index("context")
     exp = lax.axis_index("expert")
@@ -343,14 +347,43 @@
         )
         copy.start()
         g_copies.append(copy)
+    gq_copy = pltpu.make_async_copy(gq_v, gq_hbm, out_sem.at[0])
+    gq_copy.start()
     for bit in range(bits):
         g_copies[bit].wait_recv()
         gk_v[...] += grecv[bit, 0].astype(jnp.float32)
         gv_v[...] += grecv[bit, 1].astype(jnp.float32)
+    gk_copy = pltpu.make_async_copy(gk_v, gk_hbm, out_sem.at[1])
+    gk_copy.start()
+    gv_copy = pltpu.make_async_copy(gv_v, gv_hbm, out_sem.at[2])
+    gv_copy.start()
     for copy in kv_copies + x_copies + g_copies:
         copy.wait_send()
     for copy in gx_copies:
         copy.wait()
+    gq_copy.wait()
+    gk_copy.wait()
+    gv_copy.wait()
+
+
+def finish(*refs):
+    sources, results, held, sems = refs[:4], refs[4:8], refs[8:12], refs[12]
+    pieces = list(zip(sources[:3], results[:3], held[:3]))
+    for i in range(held[3].shape[0]):
+        pieces.append((sources[3].at[0, 0, i], results[3].at[0, 0, i], held[3].at[i]))
+    loads = [
+        pltpu.make_async_copy(src, mid, sems.at[0, i]) for i, (src, _, mid) in enumerate(pieces)
+    ]
+    stores = [
+        pltpu.make_async_copy(mid, dst, sems.at[1, i]) for i, (_, dst, mid) in enumerate(pieces)
+    ]
+    for load in loads:
+        load.start()
+    for load, store in zip(loads, stores):
+        load.wait()
+        store.start()
+    for store in stores:
+        store.wait()
 
 
 def solution(mesh):
@@ -423,6 +456,9 @@
             pltpu.VMEM((bits, 2, rows, kv_width), bf16),
             pltpu.VMEM((bits, 2, rows, kv_width), bf16),
             pltpu.VMEM((n_expert, cap, width), bf16),
+            pltpu.VMEM((rows, width), bf16),
+            pltpu.VMEM((rows, kv_width), f32),
+            pltpu.VMEM((rows, kv_width), f32),
             dma((len(args),)),
             dma((2 * bits,)),
             dma((2 * bits,)),
@@ -433,22 +469,39 @@
             dma((bits,)),
             dma((n_expert,)),
             dma((n_expert,)),
+            dma((3,)),
         ]
-        return pl.pallas_call(
+        outs = (
+            jax.ShapeDtypeStruct((rows, width), bf16),
+            jax.ShapeDtypeStruct((rows, kv_width), f32),
+            jax.ShapeDtypeStruct((rows, kv_width), f32),
+            jax.ShapeDtypeStruct(expert_out.shape, bf16),
+        )
+        anywhere = pl.BlockSpec(memory_space=pl.ANY)
+        done = pl.pallas_call(
             functools.partial(body, n_context, n_expert),
-            out_shape=(
-                jax.ShapeDtypeStruct((rows, width), bf16),
-                jax.ShapeDtypeStruct((rows, kv_width), f32),
-                jax.ShapeDtypeStruct((rows, kv_width), f32),
-                jax.ShapeDtypeStruct(expert_out.shape, bf16),
-            ),
-            in_specs=[pl.BlockSpec(memory_space=pltpu.HBM)] * len(args),
-            out_specs=(pl.BlockSpec(memory_space=pltpu.VMEM),) * 4,
+            out_shape=outs,
+            in_specs=[anywhere] * len(args),
+            out_specs=(anywhere,) * 4,
             scratch_shapes=scratch,
             compiler_params=pltpu.CompilerParams(
-                collective_id=0, has_side_effects=True, vmem_limit_bytes=48 * 1024 * 1024
+                collective_id=0, has_side_effects=True, vmem_limit_bytes=62 * 1024 * 1024
             ),
         )(*args)
+        return pl.pallas_call(
+            finish,
+            out_shape=outs,
+            in_specs=[anywhere] * 4,
+            out_specs=(anywhere,) * 4,
+            scratch_shapes=[
+                pltpu.VMEM((rows, width), bf16),
+                pltpu.VMEM((rows, kv_width), f32),
+                pltpu.VMEM((rows, kv_width), f32),
+                pltpu.VMEM((n_expert, cap, width), bf16),
+                dma((2, 3 + n_expert)),
+            ],
+            compiler_params=pltpu.CompilerParams(vmem_limit_bytes=62 * 1024 * 1024),
+        )(*done)
 
     rows_spec = P(("groups", "context", "expert"), "tensor")
     expert_spec = P(("groups", "context"), "expert", None, None, "tensor")

time: 60 us -> 52.7 us (0.88)
  local copies, waits for them, and re-layouts: 9.91 us -> 0 us
  Pallas kernels: 49 us -> 51.9 us
    unnamed x28 -> x0, local copies, waits for them, and re-layouts: 9.91 us -> none
    pallas_call x1 -> x2, Pallas kernels: 49 us -> 51.9 us  [the longest x1 49.9 us: local(): pl.pallas_call(functools.partial(body, n_context, n_expert), out_shape=ou...]
where the time goes in v2:
time: 52.7 us; the launch traced here: 52.6 us
  Pallas kernels  51.9 us (98%)
  between operations  0.64 us (1%)
    pallas_call x1, Pallas kernels, local(): pl.pallas_call(functools.partial(body, n_context, n_expert), out_shape=ou...  49.9 us
    pallas_call x1, Pallas kernels, local(): pl.pallas_call(finish, out_shape=outs, in_specs=[anywhere] * 4, out_specs...  2.07 us

profile of v2, /device:TPU:0, one launch (start us, length us, event | category | flops | bytes accessed | tf_op | source)
XLA Modules:
  0.0 52.6 jit_solution(4017455193971331822)
XLA Ops:
  0.6 49.9 %shard_map.147 = (bf16[128,1024]{1,0:T(8,128)(2,1)}, f32[128,256]{1,0:T(8,128)}, f32[128,256]{1,0:T(8,128)}, bf16[1,1,4,80,1024]{4,3,2,1,0:T(8,128)(2,1)}) custom-call(bf16[128,1024]{1,0:T(8,128)(2,1)} %q_hbm.1, bf16[128,256]{1,0:T(8,128)(2,1)} %k_hbm.1, bf16[128,256]{1,0:T(8,128)(2,1)} %v_hbm.1, bf16[128,1024]{1,0:T(8,128)(2,1)} %r_hbm.1, ...), custom_call_target="tpu_custom_call" | custom-call | tf_op jit(solution)/shard_map/pallas_call | solution.py:481
  50.5 2.1 %shard_map.148 = (bf16[128,1024]{1,0:T(8,128)(2,1)}, f32[128,256]{1,0:T(8,128)}, f32[128,256]{1,0:T(8,128)}, bf16[1,1,4,80,1024]{4,3,2,1,0:T(8,128)(2,1)}) custom-call(bf16[128,1024]{1,0:T(8,128)(2,1)} %get-tuple-element.8.refs_0_, f32[128,256]{1,0:T(8,128)} %get-tuple-element.9.refs_1_, f32[128,256]{1,0:T(8,128)} %get-tuple-element.10.refs_2_, ...), custom_call_target="tpu_custom_call" | custom-call | tf_op jit(solution)/shard_map/pallas_call | solution.py:491

commit v3 on v2

--- a/solution.py
+++ b/solution.py
@@ -72,6 +72,8 @@
     gsend,
     grecv,
     xsend,
+    pick_v,
+    put_v,
     gq_v,
     gk_v,
     gv_v,
@@ -109,7 +111,14 @@
             return {"expert": flipped(exp, bit)}
         return {"context": flipped(ctx, bit - e_bits)}
 
-    others = [{"expert": lax.rem(exp + off, n_expert)} for off in range(1, n_expert)]
+    def mate(distance):
+        index = exp
+        for bit in range(e_bits):
+            if distance >> bit & 1:
+                index = flipped(index, bit)
+        return index
+
+    others = [{"expert": mate(off)} for off in range(1, n_expert)]
     peers = others + [partner(bit) for bit in range(e_bits, bits)] + [{"tensor": 1 - ten}]
     barrier = pltpu.get_barrier_semaphore()
     for peer in peers:
@@ -120,7 +129,7 @@
         (k_hbm, kbuf.at[0]),
         (v_hbm, vbuf.at[0]),
         (r_hbm, r_v),
-        (x_hbm.at[0, 0, exp], xbuf.at[exp]),
+        (x_hbm.at[0, 0, exp], xbuf.at[0]),
         (routes_hbm, routes_v),
         (rw_hbm, rw_v),
         (pat_hbm, pat_s),
@@ -137,7 +146,9 @@
     pl.semaphore_wait(barrier, len(peers))
 
     kv_copies = []
-    for bit in range(bits):
+    x_copies = []
+
+    def send_kv(bit):
         for j, (src, dst) in enumerate(((k_hbm, kbuf), (v_hbm, vbuf))):
             copy = pltpu.make_async_remote_copy(
                 src_ref=src,
@@ -149,11 +160,11 @@
             )
             copy.start()
             kv_copies.append(copy)
-    x_copies = []
-    for off in range(1, n_expert):
+
+    def send_x(off):
         copy = pltpu.make_async_remote_copy(
-            src_ref=x_hbm.at[0, 0, lax.rem(exp + off, n_expert)],
-            dst_ref=xbuf.at[exp],
+            src_ref=x_hbm.at[0, 0, mate(off)],
+            dst_ref=xbuf.at[off],
             send_sem=x_send_sem.at[off],
             recv_sem=x_recv_sem.at[off],
             device_id=others[off - 1],
@@ -161,6 +172,12 @@
         )
         copy.start()
         x_copies.append(copy)
+
+    far = list(range(e_bits))[::-1]
+    for bit in far + list(range(e_bits, bits)):
+        send_kv(bit)
+    for off in range(n_expert - 1, 0, -1):
+        send_x(off)
     for copy in local:
         copy.wait()
 
@@ -177,16 +194,19 @@
     before = dot(
         member.astype(jnp.bfloat16), jnp.where(row < col, 1.0, 0.0).astype(jnp.bfloat16), NN
     )
-    slot = jnp.where(member > 0, before, -1.0).T
+    slot_row = jnp.where(member > 0, before, -1.0)
+    slot = slot_row.T
     weight = weight.T
     cap_lane = lax.broadcasted_iota(jnp.int32, (rows, cap), 1).astype(jnp.float32)
-
-    def expert_pick(index):
-        mine = lane == index
+    cap_row = lax.broadcasted_iota(jnp.int32, (cap, rows), 0).astype(jnp.float32)
+    weight_cols = []
+    for off in range(n_expert):
+        mine = lane == mate(off)
         slot_col = jnp.sum(jnp.where(mine, slot, 0.0), axis=1, keepdims=True)
-        weight_col = jnp.sum(jnp.where(mine, weight, 0.0), axis=1, keepdims=True)
-        onehot = jnp.where(slot_col == cap_lane, 1.0, 0.0).astype(jnp.bfloat16)
-        return onehot, weight_col
+        weight_cols.append(jnp.sum(jnp.where(mine, weight, 0.0), axis=1, keepdims=True))
+        one_row = jnp.sum(jnp.where(name == mate(off), slot_row, 0.0), axis=0, keepdims=True)
+        pick_v[off] = jnp.where(slot_col == cap_lane, 1.0, 0.0).astype(jnp.bfloat16)
+        put_v[off] = jnp.where(one_row == cap_row, 1.0, 0.0).astype(jnp.bfloat16)
 
     turn_row = lax.broadcasted_iota(jnp.int32, (turns, turns), 0)
     turn_col = lax.broadcasted_iota(jnp.int32, (turns, turns), 1)
@@ -250,11 +270,9 @@
 
     hid_v[...] = r_v[...].astype(jnp.float32) + attn_v[...]
     for off in range(n_expert):
-        source = lax.rem(exp - off + n_expert, n_expert)
         if off:
-            pltpu.make_async_copy(xbuf.at[source], xbuf.at[source], x_recv_sem.at[off]).wait()
-        onehot, weight_col = expert_pick(source)
-        hid_v[...] += weight_col * dot(onehot, xbuf[source], NN)
+            x_copies[-off].wait_recv()
+        hid_v[...] += weight_cols[off] * dot(pick_v[off], xbuf[off], NN)
 
     hidden = hid_v[...]
     gain = gain_v[...]
@@ -288,11 +306,9 @@
     hid_v[...] = grad_hidden
 
     gx_copies = []
-    for off in list(range(1, n_expert)) + [0]:
-        owner = lax.rem(exp + off, n_expert)
-        onehot, weight_col = expert_pick(owner)
-        weighted = (weight_col * hid_v[...]).astype(jnp.bfloat16)
-        xsend[off] = dot(onehot, weighted, TN).astype(jnp.bfloat16)
+    for off in range(n_expert - 1, -1, -1):
+        weighted = (weight_cols[off] * hid_v[...]).astype(jnp.bfloat16)
+        xsend[off] = dot(put_v[off], weighted, NN).astype(jnp.bfloat16)
         if off:
             copy = pltpu.make_async_remote_copy(
                 src_ref=xsend.at[off],
@@ -336,7 +352,7 @@
                 jnp.bfloat16
             )
     g_copies = []
-    for bit in range(bits):
+    for bit in far + list(range(e_bits, bits)):
         copy = pltpu.make_async_remote_copy(
             src_ref=gsend.at[bit],
             dst_ref=grecv.at[bit],
@@ -349,8 +365,8 @@
         g_copies.append(copy)
     gq_copy = pltpu.make_async_copy(gq_v, gq_hbm, out_sem.at[0])
     gq_copy.start()
-    for bit in range(bits):
-        g_copies[bit].wait_recv()
+    for i, bit in enumerate(far + list(range(e_bits, bits))):
+        g_copies[i].wait_recv()
         gk_v[...] += grecv[bit, 0].astype(jnp.float32)
         gv_v[...] += grecv[bit, 1].astype(jnp.float32)
     gk_copy = pltpu.make_async_copy(gk_v, gk_hbm, out_sem.at[1])
@@ -456,6 +472,8 @@
             pltpu.VMEM((bits, 2, rows, kv_width), bf16),
             pltpu.VMEM((bits, 2, rows, kv_width), bf16),
             pltpu.VMEM((n_expert, cap, width), bf16),
+            pltpu.VMEM((n_expert, rows, cap), bf16),
+            pltpu.VMEM((n_expert, cap, rows), bf16),
             pltpu.VMEM((rows, width), bf16),
             pltpu.VMEM((rows, kv_width), f32),
             pltpu.VMEM((rows, kv_width), f32),

time: 52.7 us -> 51.8 us (0.983)
  Pallas kernels: 51.9 us -> 51.1 us
    pallas_call x1, Pallas kernels: 49.9 us -> 49 us  [local(): pl.pallas_call(functools.partial(body, n_context, n_expert), out_shape=ou...]
where the time goes in v3:
time: 51.8 us; the launch traced here: 51.7 us
  Pallas kernels  51.1 us (99%)
  between operations  0.64 us (1%)
    pallas_call x1, Pallas kernels, local(): pl.pallas_call(functools.partial(body, n_context, n_expert), out_shape=ou...  49 us
    pallas_call x1, Pallas kernels, local(): pl.pallas_call(finish, out_shape=outs, in_specs=[anywhere] * 4, out_specs...  2.07 us

profile of v3, /device:TPU:0, one launch (start us, length us, event | category | flops | bytes accessed | tf_op | source)
XLA Modules:
  0.0 51.7 jit_solution(3276598396176780783)
XLA Ops:
  0.6 49.0 %shard_map.147 = (bf16[128,1024]{1,0:T(8,128)(2,1)}, f32[128,256]{1,0:T(8,128)}, f32[128,256]{1,0:T(8,128)}, bf16[1,1,4,80,1024]{4,3,2,1,0:T(8,128)(2,1)}) custom-call(bf16[128,1024]{1,0:T(8,128)(2,1)} %q_hbm.1, bf16[128,256]{1,0:T(8,128)(2,1)} %k_hbm.1, bf16[128,256]{1,0:T(8,128)(2,1)} %v_hbm.1, bf16[128,1024]{1,0:T(8,128)(2,1)} %r_hbm.1, ...), custom_call_target="tpu_custom_call" | custom-call | tf_op jit(solution)/shard_map/pallas_call | solution.py:499
  49.6 2.1 %shard_map.148 = (bf16[128,1024]{1,0:T(8,128)(2,1)}, f32[128,256]{1,0:T(8,128)}, f32[128,256]{1,0:T(8,128)}, bf16[1,1,4,80,1024]{4,3,2,1,0:T(8,128)(2,1)}) custom-call(bf16[128,1024]{1,0:T(8,128)(2,1)} %get-tuple-element.8.refs_0_, f32[128,256]{1,0:T(8,128)} %get-tuple-element.9.refs_1_, f32[128,256]{1,0:T(8,128)} %get-tuple-element.10.refs_2_, ...), custom_call_target="tpu_custom_call" | custom-call | tf_op jit(solution)/shard_map/pallas_call | solution.py:509
